TPU v7x, 32 devices: a whole 2x2x4 slice. The times are simulated.
32 devices in a mesh: grp: 2 (over x), seq: 4 (over y, core), res: 4 (over z).
Axes of the slice: x: 2, y: 2, z: 4, core: 2. Of those that a mesh axis runs over, the one named last changes fastest.
Arguments:
- alignment_features: bfloat16 [256, 256, 256], P(('grp', 'seq'), 'res'), parts along dimension 0, may hold values from -6 to 6
- scaling_coefficients: float32 [256], replicated, may hold values from 0.1 to 1.9
- first_projector: bfloat16 [256, 32], replicated, may hold values from -0.375 to 0.375
- second_projector: bfloat16 [256, 32], replicated, may hold values from -0.375 to 0.375
- final_projector: float32 [1024, 128], replicated, may hold values from -5 to 5
- final_offset: float32 [128], replicated, may hold values from -3 to 3
Outputs:
- pair: float32 [512, 256, 128], P(('grp', 'res'), 'seq'), parts along dimension 0
There are 2 independent parts, one for each index of `grp`. A program takes and returns all parts, laid end to end along the dimension named above; an argument that names none is the same for every part. Nothing has to cross between parts.
All inputs are finite; a program needn't handle non-finite values.
Results may differ from a plain program's by a relative error of at most 0.0053.
Values may be sent and summed in bfloat16 or wider, within the bound.
A program may use at most 64 MiB of HBM per device.

v0:
```python
import jax
import jax.numpy as jnp
from jax import lax
from jax.sharding import PartitionSpec as P


def standardize_rows(values, gain):
    wide = values.astype(jnp.float32)
    center = wide - jnp.mean(wide, axis=-1, keepdims=True)
    spread = jnp.mean(center * center, axis=-1, keepdims=True)
    return (center * lax.rsqrt(spread + 1e-05) * gain).astype(jnp.bfloat16)


def project_pairs(left_wide, right_wide, final_projector, scale):
    rows = left_wide.shape[1]
    cols = right_wide.shape[1]
    width = left_wide.shape[2]

    def row_block(start):
        block = lax.dynamic_slice_in_dim(left_wide, start, 4, 1)
        outer = (
            jnp.einsum("sic,sje->ijce", block, right_wide, preferred_element_type=jnp.float32)
            * scale
        )
        outer = outer.reshape(4 * cols, width * width)
        result = jnp.dot(
            outer,
            final_projector,
            precision=lax.Precision.HIGHEST,
            preferred_element_type=jnp.float32,
        )
        return result.reshape(4, cols, final_projector.shape[1])

    starts = jnp.arange(rows // 4) * 4
    return lax.map(row_block, starts).reshape(rows, cols, final_projector.shape[1])


def local(
    alignment_features,
    scaling_coefficients,
    first_projector,
    second_projector,
    final_projector,
    final_offset,
):
    aligned_portion_here, amino_portion_here, alignment_inputs = alignment_features.shape
    standardized_alignment = standardize_rows(alignment_features, scaling_coefficients).reshape(
        -1, alignment_inputs
    )
    first_factor = jnp.dot(
        standardized_alignment, first_projector, preferred_element_type=jnp.float32
    ).astype(jnp.bfloat16)
    second_factor = jnp.dot(
        standardized_alignment, second_projector, preferred_element_type=jnp.float32
    ).astype(jnp.bfloat16)
    first_factor = first_factor.reshape(aligned_portion_here, amino_portion_here, -1)
    second_factor = second_factor.reshape(aligned_portion_here, amino_portion_here, -1)
    total_seqs = aligned_portion_here * lax.axis_size("seq")
    scale = 1.0 / total_seqs
    partial_sum = project_pairs(
        first_factor,
        lax.all_gather(second_factor, "res", axis=1, tiled=True),
        final_projector,
        scale,
    )
    summed = lax.psum_scatter(partial_sum, "seq", scatter_dimension=1, tiled=True)
    return summed + final_offset


def solution(mesh):
    return jax.shard_map(
        local,
        mesh=mesh,
        in_specs=(P(("grp", "seq"), "res", None), P(), P(), P(), P(), P()),
        out_specs=P(("grp", "res"), "seq", None),
        check_vma=False,
    )
```

profile of v0, /device:TPU:1, one launch (start us, length us, event | category | flops | bytes accessed | tf_op | source)
XLA Modules:
  0.0 347.0 jit_solution(18325504904219956901)
XLA Ops:
  12.5 38.1 %all_gather.3 = bf16[32,256,32]{2,0,1:T(8,128)(2,1)} all-gather(bf16[32,64,32]{2,0,1:T(8,128)(2,1)S(1)} %copy.13), channel_id=1, replica_groups=mesh['grp'=2,'seq'=4,'res'=4] {'res'}, dimensions={1}, use_global_device_ids=true | all-gather | bytes 655360 | tf_op jit(solution)/shard_map/all_gather | solution.py:62
  50.6 3.7 %copy.15 = bf16[32,256,32]{1,0,2:T(8,128)(2,1)S(1)} copy(bf16[32,256,32]{2,0,1:T(8,128)(2,1)} %all_gather.3) | data formatting | bytes 1048576 | tf_op jit(solution)/shard_map/while | solution.py:35
  55.8 206.5 %while.10 = (s32[]{:T(128)}, f32[16,4,256,128]{3,2,1,0:T(8,128)}, s32[16]{0:T(128)S(1)}, bf16[32,64,32]{0,2,1:T(8,128)(2,1)S(1)}, bf16[32,256,32]{1,0,2:T(8,128)...) while((s32[]{:T(128)}, f32[16,4,256,128]{3,2,1,0:T(8,128)}, s32[16]{0:T(128)S(1)}, ...), condition=%wide.region_3.4_spmd, body=%wide.region_2.3_spmd.sunk | while | flops 1678770176 | bytes 18383504 | solution.py:35
  58.8 2.4 copy.19
  61.2 7.4 %fusion.25 = f32[16,4,256,128]{3,2,1,0:T(8,128)} fusion(f32[16,4,256,128]{3,2,1,0:T(8,128)} %get-tuple-element.115, s32[]{:T(128)} %get-tuple-element.114, f32[4,256,1024]{1,2,0:T(8,128)S(1)} %bitcast.46, f32[1024,128]{1,0:T(8,128)S(1)} %get-tuple-element.128), kind=kOutput, calls=%fused_computation.2.clone.1 | convolution fusion | flops 1610612736 | bytes 5243392 | tf_op jit(solution)/shard_map/while/body/eval_jaxpr/dot_general | solution.py:26
  71.7 2.4 copy.19
  74.1 7.5 %fusion.25 = f32[16,4,256,128]{3,2,1,0:T(8,128)} fusion(f32[16,4,256,128]{3,2,1,0:T(8,128)} %get-tuple-element.115, s32[]{:T(128)} %get-tuple-element.114, f32[4,256,1024]{1,2,0:T(8,128)S(1)} %bitcast.46, f32[1024,128]{1,0:T(8,128)S(1)} %get-tuple-element.128), kind=kOutput, calls=%fused_computation.2.clone.1 | convolution fusion | flops 1610612736 | bytes 5243392 | tf_op jit(solution)/shard_map/while/body/eval_jaxpr/dot_general | solution.py:26
  87.0 7.5 %fusion.25 = f32[16,4,256,128]{3,2,1,0:T(8,128)} fusion(f32[16,4,256,128]{3,2,1,0:T(8,128)} %get-tuple-element.115, s32[]{:T(128)} %get-tuple-element.114, f32[4,256,1024]{1,2,0:T(8,128)S(1)} %bitcast.46, f32[1024,128]{1,0:T(8,128)S(1)} %get-tuple-element.128), kind=kOutput, calls=%fused_computation.2.clone.1 | convolution fusion | flops 1610612736 | bytes 5243392 | tf_op jit(solution)/shard_map/while/body/eval_jaxpr/dot_general | solution.py:26
  99.9 7.5 %fusion.25 = f32[16,4,256,128]{3,2,1,0:T(8,128)} fusion(f32[16,4,256,128]{3,2,1,0:T(8,128)} %get-tuple-element.115, s32[]{:T(128)} %get-tuple-element.114, f32[4,256,1024]{1,2,0:T(8,128)S(1)} %bitcast.46, f32[1024,128]{1,0:T(8,128)S(1)} %get-tuple-element.128), kind=kOutput, calls=%fused_computation.2.clone.1 | convolution fusion | flops 1610612736 | bytes 5243392 | tf_op jit(solution)/shard_map/while/body/eval_jaxpr/dot_general | solution.py:26
  112.8 7.5 %fusion.25 = f32[16,4,256,128]{3,2,1,0:T(8,128)} fusion(f32[16,4,256,128]{3,2,1,0:T(8,128)} %get-tuple-element.115, s32[]{:T(128)} %get-tuple-element.114, f32[4,256,1024]{1,2,0:T(8,128)S(1)} %bitcast.46, f32[1024,128]{1,0:T(8,128)S(1)} %get-tuple-element.128), kind=kOutput, calls=%fused_computation.2.clone.1 | convolution fusion | flops 1610612736 | bytes 5243392 | tf_op jit(solution)/shard_map/while/body/eval_jaxpr/dot_general | solution.py:26
  125.7 7.5 %fusion.25 = f32[16,4,256,128]{3,2,1,0:T(8,128)} fusion(f32[16,4,256,128]{3,2,1,0:T(8,128)} %get-tuple-element.115, s32[]{:T(128)} %get-tuple-element.114, f32[4,256,1024]{1,2,0:T(8,128)S(1)} %bitcast.46, f32[1024,128]{1,0:T(8,128)S(1)} %get-tuple-element.128), kind=kOutput, calls=%fused_computation.2.clone.1 | convolution fusion | flops 1610612736 | bytes 5243392 | tf_op jit(solution)/shard_map/while/body/eval_jaxpr/dot_general | solution.py:26
  138.6 7.5 %fusion.25 = f32[16,4,256,128]{3,2,1,0:T(8,128)} fusion(f32[16,4,256,128]{3,2,1,0:T(8,128)} %get-tuple-element.115, s32[]{:T(128)} %get-tuple-element.114, f32[4,256,1024]{1,2,0:T(8,128)S(1)} %bitcast.46, f32[1024,128]{1,0:T(8,128)S(1)} %get-tuple-element.128), kind=kOutput, calls=%fused_computation.2.clone.1 | convolution fusion | flops 1610612736 | bytes 5243392 | tf_op jit(solution)/shard_map/while/body/eval_jaxpr/dot_general | solution.py:26
  149.1 2.4 copy.19
  151.5 7.5 %fusion.25 = f32[16,4,256,128]{3,2,1,0:T(8,128)} fusion(f32[16,4,256,128]{3,2,1,0:T(8,128)} %get-tuple-element.115, s32[]{:T(128)} %get-tuple-element.114, f32[4,256,1024]{1,2,0:T(8,128)S(1)} %bitcast.46, f32[1024,128]{1,0:T(8,128)S(1)} %get-tuple-element.128), kind=kOutput, calls=%fused_computation.2.clone.1 | convolution fusion | flops 1610612736 | bytes 5243392 | tf_op jit(solution)/shard_map/while/body/eval_jaxpr/dot_general | solution.py:26
  164.4 7.5 %fusion.25 = f32[16,4,256,128]{3,2,1,0:T(8,128)} fusion(f32[16,4,256,128]{3,2,1,0:T(8,128)} %get-tuple-element.115, s32[]{:T(128)} %get-tuple-element.114, f32[4,256,1024]{1,2,0:T(8,128)S(1)} %bitcast.46, f32[1024,128]{1,0:T(8,128)S(1)} %get-tuple-element.128), kind=kOutput, calls=%fused_computation.2.clone.1 | convolution fusion | flops 1610612736 | bytes 5243392 | tf_op jit(solution)/shard_map/while/body/eval_jaxpr/dot_general | solution.py:26
  177.3 7.5 %fusion.25 = f32[16,4,256,128]{3,2,1,0:T(8,128)} fusion(f32[16,4,256,128]{3,2,1,0:T(8,128)} %get-tuple-element.115, s32[]{:T(128)} %get-tuple-element.114, f32[4,256,1024]{1,2,0:T(8,128)S(1)} %bitcast.46, f32[1024,128]{1,0:T(8,128)S(1)} %get-tuple-element.128), kind=kOutput, calls=%fused_computation.2.clone.1 | convolution fusion | flops 1610612736 | bytes 5243392 | tf_op jit(solution)/shard_map/while/body/eval_jaxpr/dot_general | solution.py:26
  190.3 7.5 %fusion.25 = f32[16,4,256,128]{3,2,1,0:T(8,128)} fusion(f32[16,4,256,128]{3,2,1,0:T(8,128)} %get-tuple-element.115, s32[]{:T(128)} %get-tuple-element.114, f32[4,256,1024]{1,2,0:T(8,128)S(1)} %bitcast.46, f32[1024,128]{1,0:T(8,128)S(1)} %get-tuple-element.128), kind=kOutput, calls=%fused_computation.2.clone.1 | convolution fusion | flops 1610612736 | bytes 5243392 | tf_op jit(solution)/shard_map/while/body/eval_jaxpr/dot_general | solution.py:26
  203.2 7.5 %fusion.25 = f32[16,4,256,128]{3,2,1,0:T(8,128)} fusion(f32[16,4,256,128]{3,2,1,0:T(8,128)} %get-tuple-element.115, s32[]{:T(128)} %get-tuple-element.114, f32[4,256,1024]{1,2,0:T(8,128)S(1)} %bitcast.46, f32[1024,128]{1,0:T(8,128)S(1)} %get-tuple-element.128), kind=kOutput, calls=%fused_computation.2.clone.1 | convolution fusion | flops 1610612736 | bytes 5243392 | tf_op jit(solution)/shard_map/while/body/eval_jaxpr/dot_general | solution.py:26
  216.1 7.5 %fusion.25 = f32[16,4,256,128]{3,2,1,0:T(8,128)} fusion(f32[16,4,256,128]{3,2,1,0:T(8,128)} %get-tuple-element.115, s32[]{:T(128)} %get-tuple-element.114, f32[4,256,1024]{1,2,0:T(8,128)S(1)} %bitcast.46, f32[1024,128]{1,0:T(8,128)S(1)} %get-tuple-element.128), kind=kOutput, calls=%fused_computation.2.clone.1 | convolution fusion | flops 1610612736 | bytes 5243392 | tf_op jit(solution)/shard_map/while/body/eval_jaxpr/dot_general | solution.py:26
  229.0 7.5 %fusion.25 = f32[16,4,256,128]{3,2,1,0:T(8,128)} fusion(f32[16,4,256,128]{3,2,1,0:T(8,128)} %get-tuple-element.115, s32[]{:T(128)} %get-tuple-element.114, f32[4,256,1024]{1,2,0:T(8,128)S(1)} %bitcast.46, f32[1024,128]{1,0:T(8,128)S(1)} %get-tuple-element.128), kind=kOutput, calls=%fused_computation.2.clone.1 | convolution fusion | flops 1610612736 | bytes 5243392 | tf_op jit(solution)/shard_map/while/body/eval_jaxpr/dot_general | solution.py:26
  241.9 7.4 %fusion.25 = f32[16,4,256,128]{3,2,1,0:T(8,128)} fusion(f32[16,4,256,128]{3,2,1,0:T(8,128)} %get-tuple-element.115, s32[]{:T(128)} %get-tuple-element.114, f32[4,256,1024]{1,2,0:T(8,128)S(1)} %bitcast.46, f32[1024,128]{1,0:T(8,128)S(1)} %get-tuple-element.128), kind=kOutput, calls=%fused_computation.2.clone.1 | convolution fusion | flops 1610612736 | bytes 5243392 | tf_op jit(solution)/shard_map/while/body/eval_jaxpr/dot_general | solution.py:26
  254.8 7.5 %fusion.25 = f32[16,4,256,128]{3,2,1,0:T(8,128)} fusion(f32[16,4,256,128]{3,2,1,0:T(8,128)} %get-tuple-element.115, s32[]{:T(128)} %get-tuple-element.114, f32[4,256,1024]{1,2,0:T(8,128)S(1)} %bitcast.46, f32[1024,128]{1,0:T(8,128)S(1)} %get-tuple-element.128), kind=kOutput, calls=%fused_computation.2.clone.1 | convolution fusion | flops 1610612736 | bytes 5243392 | tf_op jit(solution)/shard_map/while/body/eval_jaxpr/dot_general | solution.py:26
  262.3 74.6 %reduce-scatter.2.cloned.1.call-done = f32[64,64,128]{2,1,0:T(8,128)} async-done(((f32[64,256,128]{2,1,0:T(8,128)}), f32[64,64,128]{2,1,0:T(8,128)}) %reduce-scatter.2.cloned.1.call-update) | async-done | bytes 2097168 | tf_op jit(solution)/shard_map/reduce_scatter | solution.py:66
  337.0 3.2 broadcast_add_fusion
  (72 shorter events, 59.2 us)
Async XLA Ops:
  6.5 4.3 %copy-start = (bf16[256,32]{0,1:T(8,128)(2,1)S(1)}, bf16[256,32]{0,1:T(8,128)(2,1)}, u32[]{:S(2)}) copy-start(bf16[256,32]{0,1:T(8,128)(2,1)} %param.11) | copy-start | bytes 49156
  6.5 3.6 %copy-start.2 = (bf16[32,64,256]{2,1,0:T(8,128)(2,1)S(1)}, bf16[32,64,256]{2,1,0:T(8,128)(2,1)}, u32[]{:S(2)}) copy-start(bf16[32,64,256]{2,1,0:T(8,128)(2,1)} %param.8) | copy-start | bytes 3145732
  6.5 3.6 %copy-start.4 = (f32[256]{0:T(256)S(1)}, f32[256]{0:T(256)}, u32[]{:S(2)}) copy-start(f32[256]{0:T(256)} %param.9) | copy-start | bytes 3076
  6.5 330.4 %reduce-scatter.2.cloned.1.call-start = ((), (), s32[]{:S(2)}) async-start(), calls=%async_computation.1 | async-start | bytes 10485760 | tf_op jit(solution)/shard_map/reduce_scatter | solution.py:66
  12.4 41.9 %copy-start.3 = (bf16[256,32]{0,1:T(8,128)(2,1)S(1)}, bf16[256,32]{0,1:T(8,128)(2,1)}, u32[]{:S(2)}) copy-start(bf16[256,32]{0,1:T(8,128)(2,1)} %param.10) | copy-start | bytes 49156
  50.6 5.2 %copy-start.1 = (f32[1024,128]{1,0:T(8,128)S(1)}, f32[1024,128]{1,0:T(8,128)}, u32[]{:S(2)}) copy-start(f32[1024,128]{1,0:T(8,128)} %param.12) | copy-start | bytes 1572868
  262.3 74.7 %copy-start.5 = (f32[128]{0:T(128)S(1)}, f32[128]{0:T(128)}, u32[]{:S(2)}) copy-start(f32[128]{0:T(128)} %param.13) | copy-start | bytes 1540
Sparse Core Ops, SparseCore 0:
  262.4 74.4 reduce-scatter.1
where the time goes:
time: 348 us; the launch traced here: 347 us
  matrix products  131 us (38%)
  waiting for transfers between devices  74.7 us (21%)
  local copies, waits for them, and re-layouts  54.2 us (16%)
  blocking collectives  38.1 us (11%)
  loops' own time  27.9 us (8%)
  between operations  13.5 us (4%)
  other arithmetic  7.47 us (2%)
    dot_general x16, matrix products, row_block(): jnp.dot(outer, final_projector, precision=lax.Precision.HIGHEST, preferre...  119 us
    reduce_scatter x1, waiting for transfers between devices, local(): lax.psum_scatter(partial_sum, 'seq', scatter_dimension=1, tiled=True)  74.6 us
    mul x16, local copies, waits for them, and re-layouts, row_block(): jnp.einsum('sic,sje->ijce', block, right_wide, preferred_element_type=jnp...  38.9 us
    all_gather x1, blocking collectives, local(): lax.all_gather(second_factor, 'res', axis=1, tiled=True)  38.1 us
    another operation x1, loops' own time, project_pairs(): lax.map(row_block, starts).reshape(rows, cols, final_projector.shape[1])  27.9 us
    dot_general x16, matrix products, row_block(): jnp.einsum('sic,sje->ijce', block, right_wide, preferred_element_type=jnp...  10.9 us
    dynamic_slice x16, local copies, waits for them, and re-layouts, project_pairs(): lax.map(row_block, starts).reshape(rows, cols, final_projector.shape[1])  9.41 us
  transfers between devices with their start and end apart: 1, of which 1 were waited for; matrix products, arithmetic and copies ran while one was open for 0% of the time, Pallas kernels for 0%

commit v1 on v0

v1 whole, which is shorter than its diff:
```python
import functools

import jax
import jax.numpy as jnp
from jax import lax
from jax.experimental import pallas as pl
from jax.experimental.pallas import tpu as pltpu
from jax.sharding import PartitionSpec as P

F32 = jnp.float32
BF16 = jnp.bfloat16
LANES = 128


def kernel(
    dims,
    x_ref,
    gain_ref,
    p1_ref,
    p2_ref,
    w_ref,
    off_ref,
    out_ref,
    normed,
    stacked,
    spread_proj,
    left_all,
    right_own,
    right_all,
    left_t,
    left_mat,
    right_mat,
    outer_mat,
    w_mat,
    left_send,
    left_recv,
    right_send,
    right_recv,
):
    n_seq, n_res, seqs, rows, cols, width, cz, chunk = dims
    per = LANES // width
    blocks = rows // per
    q = n_seq // n_res
    own = blocks // q
    feats = x_ref.shape[1]
    total = n_seq * seqs
    chunks = own // chunk
    half = LANES // 2
    s = lax.axis_index("seq")
    r = lax.axis_index("res")
    home = s // q

    barrier = pltpu.get_barrier_semaphore()
    for d in range(1, n_seq):
        pl.semaphore_signal(barrier, inc=1, device_id={"seq": lax.rem(s + d, n_seq)})
    for t in range(n_seq):
        @pl.when(jnp.logical_or(home != r, t != s))
        def _(t=t):
            pl.semaphore_signal(barrier, inc=1, device_id={"seq": t, "res": home})

    step = 4 * rows

    def norm_rows(i, carry):
        at = pl.ds(pl.multiple_of(i * step, step), step)
        wide = x_ref[at, :].astype(F32)
        center = wide - jnp.mean(wide, axis=-1, keepdims=True)
        spread = jnp.mean(center * center, axis=-1, keepdims=True)
        value = center * lax.rsqrt(spread + 1e-05) * gain_ref[...]
        normed[0, at, :] = value[:, :LANES]
        normed[1, at, :] = value[:, LANES:]
        return carry

    lax.fori_loop(0, seqs * rows // step, norm_rows, 0)

    tile_row = lax.broadcasted_iota(jnp.int32, (width, LANES), 0)
    tile_lane = lax.broadcasted_iota(jnp.int32, (width, LANES), 1)
    tiler = jnp.where(tile_lane % width == tile_row, 1.0, 0.0).astype(BF16)
    wide1 = jnp.dot(p1_ref[...], tiler, preferred_element_type=F32)
    wide2 = jnp.dot(p2_ref[...], tiler, preferred_element_type=F32)
    lane = lax.broadcasted_iota(jnp.int32, (feats, LANES), 1) // width
    for k in range(per):
        at = slice(k * feats, (k + 1) * feats)
        spread_proj[at, :LANES] = jnp.where(lane == k, wide1, 0.0).astype(BF16)
        spread_proj[at, LANES:] = jnp.where(lane == k, wide2, 0.0).astype(BF16)
    for g in range(blocks):
        for k in range(per):
            for h in range(feats // LANES):
                stacked[
                    g * seqs : (g + 1) * seqs, k * feats + h * LANES : k * feats + (h + 1) * LANES
                ] = normed[h, pl.ds(per * g + k, seqs, stride=rows), :].astype(BF16)
    both = jnp.dot(stacked[...], spread_proj[...], preferred_element_type=F32).astype(BF16)
    left_all[s] = both[:, :LANES].reshape(blocks, seqs, LANES)
    right_own[...] = both[:, LANES:].reshape(q * chunks, chunk, seqs, LANES)

    same = jnp.where(home == r, 1, 0)
    pl.semaphore_wait(barrier, n_seq - 1 + q * n_res - same)

    def left_copy(d, source):
        return pltpu.make_async_remote_copy(
            src_ref=left_all.at[source],
            dst_ref=left_all.at[source],
            send_sem=left_send.at[d],
            recv_sem=left_recv.at[source],
            device_id={"seq": lax.rem(s + d, n_seq)},
        )

    def right_copy(b, t, c, source):
        return pltpu.make_async_remote_copy(
            src_ref=right_own.at[b * chunks + c],
            dst_ref=right_all.at[c, source],
            send_sem=right_send.at[b * n_res + t, c],
            recv_sem=right_recv.at[source, c],
            device_id={"seq": r * q + b, "res": t},
        )

    def right_local(b, c):
        return pltpu.make_async_copy(
            right_own.at[b * chunks + c], right_all.at[c, s], right_recv.at[s, c]
        )

    for c in range(chunks):
        for b in range(q):
            for t in range(n_res):
                mine = jnp.logical_and(r * q + b == s, t == r)

                @pl.when(jnp.logical_not(mine))
                def _(b=b, t=t, c=c):
                    right_copy(b, t, c, s).start()

                @pl.when(mine)
                def _(b=b, c=c):
                    right_local(b, c).start()

        if c == 0:
            for d in range(1, n_seq):
                left_copy(d, s).start()

    for c in range(width):
        part = w_ref[c * width : (c + 1) * width, :].astype(BF16)
        zero = jnp.zeros((width, cz), BF16)
        w_mat[2 * c * width : (2 * c + 1) * width, :cz] = part
        w_mat[2 * c * width : (2 * c + 1) * width, cz:] = zero
        w_mat[(2 * c + 1) * width : (2 * c + 2) * width, :cz] = zero
        w_mat[(2 * c + 1) * width : (2 * c + 2) * width, cz:] = part

    for d in range(1, n_seq):
        left_copy(d, lax.rem(s + n_seq - d, n_seq)).wait_recv()
    for g in range(blocks):
        block = left_all[:, g].reshape(total, LANES).astype(F32)
        left_t[:, g * LANES : (g + 1) * LANES, :] = (
            block.T.reshape(LANES, total // LANES, LANES).transpose(1, 0, 2)
            if total > LANES
            else block.T[None]
        )
    for c in range(width):
        for h in range(total // LANES):
            left_mat[
                (c // 2) * rows : (c // 2 + 1) * rows,
                (c % 2) * total + h * LANES : (c % 2) * total + (h + 1) * LANES,
            ] = left_t[h, pl.ds(c, rows, stride=width), :].astype(BF16)

    low = lax.broadcasted_iota(jnp.int32, (total, LANES), 1) < half
    scale = 1.0 / total
    for c in range(chunks):
        for t in range(n_seq):
            right_copy(0, 0, c, t).wait_recv()
        for g in range(chunk):
            block = right_all[c, :, g].reshape(total, LANES).astype(F32)
            turned = pltpu.roll(block, half, 1)
            right_mat[:total, :LANES] = jnp.where(low, block, 0.0).astype(BF16)
            right_mat[total:, :LANES] = jnp.where(low, 0.0, turned).astype(BF16)
            right_mat[:total, LANES:] = jnp.where(low, turned, 0.0).astype(BF16)
            right_mat[total:, LANES:] = jnp.where(low, 0.0, block).astype(BF16)
            outer = jnp.dot(left_mat[...], right_mat[...], preferred_element_type=F32).astype(BF16)
            for h in range(2):
                for p in range(width // 2):
                    outer_mat[
                        (2 * g + h) * rows : (2 * g + h + 1) * rows, p * LANES : (p + 1) * LANES
                    ] = outer[p * rows : (p + 1) * rows, h * LANES : (h + 1) * LANES]
        result = jnp.dot(outer_mat[...], w_mat[...], preferred_element_type=F32)
        for p in range(2 * chunk):
            for h in range(2):
                col = (c * chunk * 2 + p) * 2 + h
                out_ref[pl.ds(col, rows, stride=cols), :] = (
                    result[p * rows : (p + 1) * rows, h * cz : (h + 1) * cz] * scale + off_ref[...]
                )

    for d in range(1, n_seq):
        left_copy(d, s).wait_send()
    for c in range(chunks):
        for b in range(q):
            for t in range(n_res):
                mine = jnp.logical_and(r * q + b == s, t == r)

                @pl.when(jnp.logical_not(mine))
                def _(b=b, t=t, c=c):
                    right_copy(b, t, c, s).wait_send()


def local(n_seq, n_res, features, gain, p1, p2, w, offset):
    seqs, rows, feats = features.shape
    width = p1.shape[1]
    cz = w.shape[1]
    cols = rows * n_res // n_seq
    per = LANES // width
    blocks = rows // per
    q = n_seq // n_res
    own = blocks // q
    chunk = 4
    chunks = own // chunk
    total = n_seq * seqs
    dims = (n_seq, n_res, seqs, rows, cols, width, cz, chunk)
    vmem = pl.BlockSpec(memory_space=pltpu.VMEM)
    out = pl.pallas_call(
        functools.partial(kernel, dims),
        out_shape=jax.ShapeDtypeStruct((rows * cols, cz), F32),
        in_specs=[vmem] * 6,
        out_specs=vmem,
        scratch_shapes=[
            pltpu.VMEM((feats // LANES, seqs * rows, LANES), F32),
            pltpu.VMEM((blocks * seqs, per * feats), BF16),
            pltpu.VMEM((per * feats, 2 * LANES), BF16),
            pltpu.VMEM((n_seq, blocks, seqs, LANES), BF16),
            pltpu.VMEM((q * chunks, chunk, seqs, LANES), BF16),
            pltpu.VMEM((chunks, n_seq, chunk, seqs, LANES), BF16),
            pltpu.VMEM((total // LANES, rows * width, LANES), F32),
            pltpu.VMEM((width // 2 * rows, 2 * total), BF16),
            pltpu.VMEM((2 * total, 2 * LANES), BF16),
            pltpu.VMEM((chunk * 2 * rows, width // 2 * LANES), BF16),
            pltpu.VMEM((2 * width * width, 2 * cz), BF16),
            pltpu.SemaphoreType.DMA((n_seq,)),
            pltpu.SemaphoreType.DMA((n_seq,)),
            pltpu.SemaphoreType.DMA((n_seq, chunks)),
            pltpu.SemaphoreType.DMA((n_seq, chunks)),
        ],
        compiler_params=pltpu.CompilerParams(
            collective_id=0, has_side_effects=True, vmem_limit_bytes=48 * 1024 * 1024
        ),
    )(
        features.reshape(seqs * rows, feats),
        gain.reshape(1, feats),
        p1,
        p2,
        w,
        offset.reshape(1, cz),
    )
    return out.reshape(rows, cols, cz)


def solution(mesh):
    return jax.shard_map(
        functools.partial(local, mesh.shape["seq"], mesh.shape["res"]),
        mesh=mesh,
        in_specs=(P(("grp", "seq"), "res", None), P(), P(), P(), P(), P()),
        out_specs=P(("grp", "res"), "seq", None),
        check_vma=False,
    )
```

time: 348 us -> 35.2 us (0.10)
  matrix products: 131 us -> 0 us
  waiting for transfers between devices: 74.7 us -> 0 us
  local copies, waits for them, and re-layouts: 54.2 us -> 6.59 us
  blocking collectives: 38.1 us -> 0 us
  Pallas kernels: 0 us -> 28.1 us
  loops' own time: 27.9 us -> 0 us
  between operations: 13.5 us -> 0.02 us
  other arithmetic: 7.47 us -> 0 us
    dot_general x34 -> x0, matrix products: 131 us -> none  [the longest x16 119 us: row_block(): jnp.dot(outer, final_projector, precision=lax.Precision.HIGHEST, preferre...]
    reduce_scatter x1 -> x0, waiting for transfers between devices: 74.6 us -> none  [local(): lax.psum_scatter(partial_sum, 'seq', scatter_dimension=1, tiled=True)]
    mul x16 -> x0, local copies, waits for them, and re-layouts: 38.9 us -> none  [row_block(): jnp.einsum('sic,sje->ijce', block, right_wide, preferred_element_type=jnp...]
    all_gather x1 -> x0, blocking collectives: 38.1 us -> none  [local(): lax.all_gather(second_factor, 'res', axis=1, tiled=True)]
    pallas_call x0 -> x1, Pallas kernels: none -> 28.1 us  [local(): pl.pallas_call(functools.partial(kernel, dims), out_shape=jax.ShapeDtypeS...]
    another operation x1 -> x0, loops' own time: 27.9 us -> none  [project_pairs(): lax.map(row_block, starts).reshape(rows, cols, final_projector.shape[1])]
    dynamic_slice x16 -> x0, local copies, waits for them, and re-layouts: 9.41 us -> none  [project_pairs(): lax.map(row_block, starts).reshape(rows, cols, final_projector.shape[1])]
    unnamed x12 -> x11, local copies, waits for them, and re-layouts: 0.03 us -> 6.59 us
  transfers between devices with their start and end apart: 1 -> 0, of which waited for: 1 -> 0; matrix products, arithmetic and copies ran while one was open for 0% -> 0% of each run, Pallas kernels for 0% -> 0%
where the time goes in v1:
time: 35.2 us; the launch traced here: 34.7 us
  Pallas kernels  28.1 us (80%)
  local copies, waits for them, and re-layouts  6.59 us (19%)
    pallas_call x1, Pallas kernels, local(): pl.pallas_call(functools.partial(kernel, dims), out_shape=jax.ShapeDtypeS...  28.1 us
    unnamed x11, local copies, waits for them, and re-layouts  6.59 us

profile of v1, /device:TPU:1, one launch (start us, length us, event | category | flops | bytes accessed | tf_op | source)
XLA Modules:
  0.0 34.7 jit_solution(8402491722309006755)
XLA Ops:
  0.0 0.8 %copy.7.p1_ref = bf16[256,32]{1,0:T(8,128)(2,1)S(1)} copy(bf16[256,32]{0,1:T(8,128)(2,1)} %param.8) | data formatting | bytes 32768 | tf_op args[2]
  0.8 0.8 %copy.8.p2_ref = bf16[256,32]{1,0:T(8,128)(2,1)S(1)} copy(bf16[256,32]{0,1:T(8,128)(2,1)} %param.9) | data formatting | bytes 32768 | tf_op args[3]
  1.7 0.0 copy-start
  1.7 1.2 %copy-done = bf16[32,64,256]{2,1,0:T(8,128)(2,1)S(1)} copy-done((bf16[32,64,256]{2,1,0:T(8,128)(2,1)S(1)}, bf16[32,64,256]{2,1,0:T(8,128)(2,1)}, u32[]{:S(2)}) %copy-start) | copy-done | bytes 1048600
  2.9 0.0 copy-start.1
  2.9 1.0 %copy-done.1 = f32[1024,128]{1,0:T(8,128)S(1)} copy-done((f32[1024,128]{1,0:T(8,128)S(1)}, f32[1024,128]{1,0:T(8,128)}, u32[]{:S(2)}) %copy-start.1) | copy-done | bytes 524312
  3.9 0.0 copy-start.2
  3.9 0.7 %copy-done.2 = f32[256]{0:T(256)S(1)} copy-done((f32[256]{0:T(256)S(1)}, f32[256]{0:T(256)}, u32[]{:S(2)}) %copy-start.2) | copy-done | bytes 1048
  4.6 0.0 copy-start.3
  4.6 0.7 %copy-done.3 = f32[128]{0:T(128)S(1)} copy-done((f32[128]{0:T(128)S(1)}, f32[128]{0:T(128)}, u32[]{:S(2)}) %copy-start.3) | copy-done | bytes 536
  5.3 28.1 %shard_map.64 = f32[4096,128]{1,0:T(8,128)S(1)} custom-call(bf16[2048,256]{1,0:T(8,128)(2,1)S(1)} %bitcast.5, f32[1,256]{1,0:T(1,128)S(1)} %bitcast.6, bf16[256,32]{1,0:T(8,128)(2,1)S(1)} %copy.7.p1_ref, bf16[256,32]{1,0:T(8,128)(2,1)S(1)} %copy.8.p2_ref, f32[1024,128]{1,0:T(8,128)S(1)} %copy-done.1, f32[1,128]{1,0:T(1,128)S(1)} %bitcast.7), custom_call_target="tpu_custom_call" | custom-call | tf_op jit(solution)/shard_map/pallas_call | solution.py:214
  33.4 1.3 %copy.10 = f32[64,64,128]{2,1,0:T(8,128)} copy(f32[64,64,128]{2,1,0:T(8,128)S(1)} %bitcast.4) | data formatting | bytes 4194304
Async XLA Ops:
  1.7 1.2 %copy-start = (bf16[32,64,256]{2,1,0:T(8,128)(2,1)S(1)}, bf16[32,64,256]{2,1,0:T(8,128)(2,1)}, u32[]{:S(2)}) copy-start(bf16[32,64,256]{2,1,0:T(8,128)(2,1)} %param.6) | copy-start | bytes 3145732
  2.9 1.0 %copy-start.1 = (f32[1024,128]{1,0:T(8,128)S(1)}, f32[1024,128]{1,0:T(8,128)}, u32[]{:S(2)}) copy-start(f32[1024,128]{1,0:T(8,128)} %w_ref.1) | copy-start | bytes 1572868
  3.9 0.7 %copy-start.2 = (f32[256]{0:T(256)S(1)}, f32[256]{0:T(256)}, u32[]{:S(2)}) copy-start(f32[256]{0:T(256)} %param.7) | copy-start | bytes 3076
  4.6 0.7 %copy-start.3 = (f32[128]{0:T(128)S(1)}, f32[128]{0:T(128)}, u32[]{:S(2)}) copy-start(f32[128]{0:T(128)} %param.11) | copy-start | bytes 1540

commit v2 on v1

v2 whole, which is shorter than its diff:
```python
import functools

import jax
import jax.numpy as jnp
from jax import lax
from jax.experimental import pallas as pl
from jax.experimental.pallas import tpu as pltpu
from jax.sharding import PartitionSpec as P

F32 = jnp.float32
BF16 = jnp.bfloat16
LANES = 128


def kernel(
    dims,
    x_ref,
    gain_ref,
    p1_ref,
    p2_ref,
    w_ref,
    off_ref,
    out_ref,
    x_in,
    gain_in,
    p1_in,
    p2_in,
    w_in,
    off_in,
    normed,
    stacked,
    spread_proj,
    left_all,
    right_own,
    right_all,
    left_t,
    left_mat,
    right_mat,
    outer_mat,
    w_mat,
    left_send,
    left_recv,
    right_send,
    right_recv,
    x_sem,
    in_sem,
):
    n_seq, n_res, seqs, rows, cols, width, cz, chunk = dims
    per = LANES // width
    blocks = rows // per
    q = n_seq // n_res
    own = blocks // q
    feats = x_ref.shape[2]
    total = n_seq * seqs
    chunks = own // chunk
    parts = blocks // chunk
    some = per * chunk
    half = LANES // 2
    s = lax.axis_index("seq")
    r = lax.axis_index("res")
    home = s // q

    def x_copy(k):
        at = (slice(None), slice(k * some, (k + 1) * some))
        return pltpu.make_async_copy(x_ref.at[at], x_in.at[at], x_sem.at[k])

    small = [
        pltpu.make_async_copy(a, b, in_sem.at[n])
        for n, (a, b) in enumerate(
            [
                (p1_ref, p1_in),
                (p2_ref, p2_in),
                (gain_ref, gain_in),
                (off_ref, off_in),
                (w_ref, w_in),
            ]
        )
    ]
    x_copy(0).start()
    for copy in small[:4]:
        copy.start()
    for k in range(1, parts):
        x_copy(k).start()
    small[4].start()

    barrier = pltpu.get_barrier_semaphore()
    for d in range(1, n_seq):
        pl.semaphore_signal(barrier, inc=1, device_id={"seq": lax.rem(s + d, n_seq)})
    for t in range(n_seq):
        @pl.when(jnp.logical_or(home != r, t != s))
        def _(t=t):
            pl.semaphore_signal(barrier, inc=1, device_id={"seq": t, "res": home})

    def left_copy(d, k, source):
        return pltpu.make_async_remote_copy(
            src_ref=left_all.at[k, source],
            dst_ref=left_all.at[k, source],
            send_sem=left_send.at[d, k],
            recv_sem=left_recv.at[source, k],
            device_id={"seq": lax.rem(s + d, n_seq)},
        )

    def left_pass(d, k, source):
        return pltpu.make_async_remote_copy(
            src_ref=left_all.at[k, source],
            dst_ref=left_all.at[k, source],
            send_sem=left_send.at[d + 1, k],
            recv_sem=left_recv.at[source, k],
            device_id={"seq": s + 1 - 2 * lax.rem(s, 2)},
        )

    def right_copy(b, t, c, source):
        return pltpu.make_async_remote_copy(
            src_ref=right_own.at[b * chunks + c],
            dst_ref=right_all.at[c, source],
            send_sem=right_send.at[b * n_res + t, c],
            recv_sem=right_recv.at[source, c],
            device_id={"seq": r * q + b, "res": t},
        )

    def right_local(b, c):
        return pltpu.make_async_copy(
            right_own.at[b * chunks + c], right_all.at[c, s], right_recv.at[s, c]
        )

    def right_start(k):
        b, c = k // chunks, k % chunks
        for t in range(n_res):
            mine = jnp.logical_and(r * q + b == s, t == r)

            @pl.when(jnp.logical_not(mine))
            def _(t=t):
                right_copy(b, t, c, s).start()

            @pl.when(mine)
            def _():
                right_local(b, c).start()

    def right_sent(k):
        b, c = k // chunks, k % chunks
        for t in range(n_res):
            mine = jnp.logical_and(r * q + b == s, t == r)

            @pl.when(jnp.logical_not(mine))
            def _(t=t):
                right_copy(b, t, c, s).wait_send()

    for copy in small[:3]:
        copy.wait()
    tile_row = lax.broadcasted_iota(jnp.int32, (width, LANES), 0)
    tile_lane = lax.broadcasted_iota(jnp.int32, (width, LANES), 1)
    tiler = jnp.where(tile_lane % width == tile_row, 1.0, 0.0).astype(BF16)
    first = (((0,), (0,)), ((), ()))
    wide1 = lax.dot_general(p1_in[...], tiler, first, preferred_element_type=F32)
    wide2 = lax.dot_general(p2_in[...], tiler, first, preferred_element_type=F32)
    lane = lax.broadcasted_iota(jnp.int32, (feats, LANES), 1) // width
    for k in range(per):
        at = slice(k * feats, (k + 1) * feats)
        spread_proj[at, :LANES] = jnp.where(lane == k, wide1, 0.0).astype(BF16)
        spread_proj[at, LANES:] = jnp.where(lane == k, wide2, 0.0).astype(BF16)

    same = jnp.where(home == r, 1, 0)
    step = 8
    gain = gain_in[...]
    ones = jnp.ones((feats, feats), BF16)
    for k in range(parts):
        x_copy(k).wait()
        for n in range(seqs // step):
            block = x_in[n * step : (n + 1) * step, k * some : (k + 1) * some, :]
            wide = block.reshape(step * some, feats).astype(F32)
            rowsum = jnp.dot(block.reshape(step * some, feats), ones, preferred_element_type=F32)
            center = wide - rowsum * (1.0 / feats)
            square = center * center
            high = square.astype(BF16)
            rest = (square - high.astype(F32)).astype(BF16)
            spread = jnp.dot(high, ones, preferred_element_type=F32) + jnp.dot(
                rest, ones, preferred_element_type=F32
            )
            value = center * lax.rsqrt(spread * (1.0 / feats) + 1e-05) * gain
            for h in range(feats // LANES):
                normed[k, h, n * step * some : (n + 1) * step * some, :] = value[
                    :, h * LANES : (h + 1) * LANES
                ]
        for g in range(chunk):
            for j in range(per):
                for h in range(feats // LANES):
                    at = j * feats + h * LANES
                    stacked[k, g * seqs : (g + 1) * seqs, at : at + LANES] = normed[
                        k, h, pl.ds(per * g + j, seqs, stride=some), :
                    ].astype(BF16)
        both = jnp.dot(stacked[k], spread_proj[...], preferred_element_type=F32).astype(BF16)
        left_all[k, s] = both[:, :LANES].reshape(chunk, seqs, LANES)
        right_own[k] = both[:, LANES:].reshape(chunk, seqs, LANES)
        if k == 0:
            pl.semaphore_wait(barrier, n_seq - 1 + q * n_res - same)
        for d in range(2, n_seq, 2):
            left_copy(d, k, s).start()
        left_pass(0, k, s).start()
        if k < 2:
            right_start(k)

    small[3].wait()
    small[4].wait()
    zero = jnp.zeros((width, cz), BF16)
    for c in range(width):
        part = w_in[c * width : (c + 1) * width, :].astype(BF16)
        w_mat[2 * c * width : (2 * c + 1) * width, :cz] = part
        w_mat[2 * c * width : (2 * c + 1) * width, cz:] = zero
        w_mat[(2 * c + 1) * width : (2 * c + 2) * width, :cz] = zero
        w_mat[(2 * c + 1) * width : (2 * c + 2) * width, cz:] = part

    for k in range(parts):
        for d in range(2, n_seq, 2):
            source = lax.rem(s + n_seq - d, n_seq)
            left_copy(d, k, source).wait_recv()
            left_pass(d, k, source).start()
    for k in range(2, parts):
        right_sent(k - 2)
        right_start(k)
    for k in range(parts):
        for d in range(0, n_seq, 2):
            left_copy(0, k, lax.rem(s + 1 - 2 * lax.rem(s, 2) + n_seq - d, n_seq)).wait_recv()
        for g in range(chunk):
            block = left_all[k, :, g].reshape(total, LANES).astype(F32).T
            for h in range(total // LANES):
                at = (k * chunk + g) * LANES
                left_t[h, at : at + LANES, :] = block[:, h * LANES : (h + 1) * LANES]
    for c in range(width):
        for h in range(total // LANES):
            left_mat[
                (c // 2) * rows : (c // 2 + 1) * rows,
                (c % 2) * total + h * LANES : (c % 2) * total + (h + 1) * LANES,
            ] = left_t[h, pl.ds(c, rows, stride=width), :].astype(BF16)
    low = lax.broadcasted_iota(jnp.int32, (total, LANES), 1) < half
    scale = 1.0 / total
    for c in range(chunks):
        for t in range(n_seq):
            right_copy(0, 0, c, t).wait_recv()
        for g in range(chunk):
            block = right_all[c, :, g].reshape(total, LANES).astype(F32)
            turned = pltpu.roll(block, half, 1)
            right_mat[:total, :LANES] = jnp.where(low, block, 0.0).astype(BF16)
            right_mat[total:, :LANES] = jnp.where(low, 0.0, turned).astype(BF16)
            right_mat[:total, LANES:] = jnp.where(low, turned, 0.0).astype(BF16)
            right_mat[total:, LANES:] = jnp.where(low, 0.0, block).astype(BF16)
            outer = jnp.dot(left_mat[...], right_mat[...], preferred_element_type=F32).astype(BF16)
            for h in range(2):
                for p in range(width // 2):
                    outer_mat[
                        (2 * g + h) * rows : (2 * g + h + 1) * rows, p * LANES : (p + 1) * LANES
                    ] = outer[p * rows : (p + 1) * rows, h * LANES : (h + 1) * LANES]
        result = jnp.dot(outer_mat[...], w_mat[...], preferred_element_type=F32)
        for p in range(2 * chunk):
            for h in range(2):
                col = (c * chunk * 2 + p) * 2 + h
                out_ref[pl.ds(col, rows, stride=cols), :] = (
                    result[p * rows : (p + 1) * rows, h * cz : (h + 1) * cz] * scale + off_in[...]
                )

    for k in range(parts):
        for d in range(2, n_seq, 2):
            left_copy(d, k, s).wait_send()
        for d in range(0, n_seq, 2):
            left_pass(d, k, s).wait_send()
    for k in range(max(parts - 2, 0), parts):
        right_sent(k)


def local(n_seq, n_res, features, gain, p1, p2, w, offset):
    seqs, rows, feats = features.shape
    width = p1.shape[1]
    cz = w.shape[1]
    cols = rows * n_res // n_seq
    per = LANES // width
    blocks = rows // per
    q = n_seq // n_res
    own = blocks // q
    chunk = 4
    chunks = own // chunk
    total = n_seq * seqs
    dims = (n_seq, n_res, seqs, rows, cols, width, cz, chunk)
    parts = blocks // chunk
    hbm = pl.BlockSpec(memory_space=pltpu.HBM)
    out = pl.pallas_call(
        functools.partial(kernel, dims),
        out_shape=jax.ShapeDtypeStruct((rows * cols, cz), F32),
        in_specs=[hbm] * 6,
        out_specs=pl.BlockSpec(memory_space=pltpu.VMEM),
        scratch_shapes=[
            pltpu.VMEM((seqs, rows, feats), BF16),
            pltpu.VMEM((1, feats), F32),
            pltpu.VMEM((width, feats), BF16),
            pltpu.VMEM((width, feats), BF16),
            pltpu.VMEM(w.shape, F32),
            pltpu.VMEM((1, cz), F32),
            pltpu.VMEM((parts, feats // LANES, seqs * per * chunk, LANES), F32),
            pltpu.VMEM((parts, chunk * seqs, per * feats), BF16),
            pltpu.VMEM((per * feats, 2 * LANES), BF16),
            pltpu.VMEM((parts, n_seq, chunk, seqs, LANES), BF16),
            pltpu.VMEM((parts, chunk, seqs, LANES), BF16),
            pltpu.VMEM((chunks, n_seq, chunk, seqs, LANES), BF16),
            pltpu.VMEM((total // LANES, rows * width, LANES), F32),
            pltpu.VMEM((width // 2 * rows, 2 * total), BF16),
            pltpu.VMEM((2 * total, 2 * LANES), BF16),
            pltpu.VMEM((chunk * 2 * rows, width // 2 * LANES), BF16),
            pltpu.VMEM((2 * width * width, 2 * cz), BF16),
            pltpu.SemaphoreType.DMA((n_seq, parts)),
            pltpu.SemaphoreType.DMA((n_seq, parts)),
            pltpu.SemaphoreType.DMA((n_seq, chunks)),
            pltpu.SemaphoreType.DMA((n_seq, chunks)),
            pltpu.SemaphoreType.DMA((parts,)),
            pltpu.SemaphoreType.DMA((5,)),
        ],
        compiler_params=pltpu.CompilerParams(
            collective_id=0, has_side_effects=True, vmem_limit_bytes=62 * 1024 * 1024
        ),
    )(features, gain.reshape(1, feats), p1.T, p2.T, w, offset.reshape(1, cz))
    return out.reshape(rows, cols, cz)


def solution(mesh):
    return jax.shard_map(
        functools.partial(local, mesh.shape["seq"], mesh.shape["res"]),
        mesh=mesh,
        in_specs=(P(("grp", "seq"), "res", None), P(), P(), P(), P(), P()),
        out_specs=P(("grp", "res"), "seq", None),
        check_vma=False,
    )
```

time: 35.2 us -> 30.5 us (0.87)
  local copies, waits for them, and re-layouts: 6.59 us -> 3.16 us
  Pallas kernels: 28.1 us -> 27.1 us
    unnamed x11 -> x1, local copies, waits for them, and re-layouts: 6.59 us -> 3.16 us
    pallas_call x1, Pallas kernels: 28.1 us -> 27.1 us  [local(): pl.pallas_call(functools.partial(kernel, dims), out_shape=jax.ShapeDtypeS...]
where the time goes in v2:
time: 30.5 us; the launch traced here: 30.3 us
  Pallas kernels  27.1 us (89%)
  local copies, waits for them, and re-layouts  3.16 us (10%)
    pallas_call x1, Pallas kernels, local(): pl.pallas_call(functools.partial(kernel, dims), out_shape=jax.ShapeDtypeS...  27.1 us
    unnamed x1, local copies, waits for them, and re-layouts  3.16 us

profile of v2, /device:TPU:1, one launch (start us, length us, event | category | flops | bytes accessed | tf_op | source)
XLA Modules:
  0.0 30.3 jit_solution(2984332505696826694)
XLA Ops:
  0.0 27.1 %shard_map.64 = f32[4096,128]{1,0:T(8,128)} custom-call(bf16[32,64,256]{2,1,0:T(8,128)(2,1)} %x_ref.1, f32[1,256]{1,0:T(1,128)} %bitcast.8, bf16[32,256]{1,0:T(8,128)(2,1)} %bitcast.6, bf16[32,256]{1,0:T(8,128)(2,1)} %bitcast.7, f32[1024,128]{1,0:T(8,128)} %w_ref.1, f32[1,128]{1,0:T(1,128)} %bitcast.9), custom_call_target="tpu_custom_call" | custom-call | tf_op jit(solution)/shard_map/pallas_call | solution.py:284
  27.1 3.2 %copy.8 = f32[64,64,128]{2,1,0:T(8,128)} copy(f32[64,64,128]{2,1,0:T(8,128)} %bitcast.5) | data formatting | bytes 4194304

commit v3 on v2

--- a/solution.py
+++ b/solution.py
@@ -18,26 +18,18 @@
     gain_ref,
     p1_ref,
     p2_ref,
-    w_ref,
-    off_ref,
-    out_ref,
+    left_mat,
+    right_all,
     x_in,
     gain_in,
     p1_in,
     p2_in,
-    w_in,
-    off_in,
     normed,
     stacked,
     spread_proj,
     left_all,
     right_own,
-    right_all,
     left_t,
-    left_mat,
-    right_mat,
-    outer_mat,
-    w_mat,
     left_send,
     left_recv,
     right_send,
@@ -71,17 +63,14 @@
                 (p1_ref, p1_in),
                 (p2_ref, p2_in),
                 (gain_ref, gain_in),
-                (off_ref, off_in),
-                (w_ref, w_in),
             ]
         )
     ]
     x_copy(0).start()
-    for copy in small[:4]:
+    for copy in small:
         copy.start()
     for k in range(1, parts):
         x_copy(k).start()
-    small[4].start()
 
     barrier = pltpu.get_barrier_semaphore()
     for d in range(1, n_seq):
@@ -145,7 +134,7 @@
             def _(t=t):
                 right_copy(b, t, c, s).wait_send()
 
-    for copy in small[:3]:
+    for copy in small:
         copy.wait()
     tile_row = lax.broadcasted_iota(jnp.int32, (width, LANES), 0)
     tile_lane = lax.broadcasted_iota(jnp.int32, (width, LANES), 1)
@@ -199,16 +188,6 @@
         if k < 2:
             right_start(k)
 
-    small[3].wait()
-    small[4].wait()
-    zero = jnp.zeros((width, cz), BF16)
-    for c in range(width):
-        part = w_in[c * width : (c + 1) * width, :].astype(BF16)
-        w_mat[2 * c * width : (2 * c + 1) * width, :cz] = part
-        w_mat[2 * c * width : (2 * c + 1) * width, cz:] = zero
-        w_mat[(2 * c + 1) * width : (2 * c + 2) * width, :cz] = zero
-        w_mat[(2 * c + 1) * width : (2 * c + 2) * width, cz:] = part
-
     for k in range(parts):
         for d in range(2, n_seq, 2):
             source = lax.rem(s + n_seq - d, n_seq)
@@ -231,11 +210,71 @@
                 (c // 2) * rows : (c // 2 + 1) * rows,
                 (c % 2) * total + h * LANES : (c % 2) * total + (h + 1) * LANES,
             ] = left_t[h, pl.ds(c, rows, stride=width), :].astype(BF16)
+    for c in range(chunks):
+        for t in range(n_seq):
+            right_copy(0, 0, c, t).wait_recv()
+    for k in range(parts):
+        for d in range(2, n_seq, 2):
+            left_copy(d, k, s).wait_send()
+        for d in range(0, n_seq, 2):
+            left_pass(d, k, s).wait_send()
+    for k in range(max(parts - 2, 0), parts):
+        right_sent(k)
+
+
+def pair_kernel(
+    dims,
+    left_hbm,
+    right_hbm,
+    w_hbm,
+    off_hbm,
+    out_ref,
+    left_mat,
+    right_all,
+    w_ref,
+    off_ref,
+    right_mat,
+    outer_mat,
+    w_mat,
+    out_buf,
+    sem,
+    in_sem,
+):
+    n_seq, n_res, seqs, rows, cols, width, cz, chunk = dims
+    chunks = right_all.shape[0]
+    total = n_seq * seqs
+    half = LANES // 2
+    some = cols // chunks
+    arrive = [
+        pltpu.make_async_copy(a, b, in_sem.at[n])
+        for n, (a, b) in enumerate(
+            [(w_hbm, w_ref), (left_hbm, left_mat), (right_hbm, right_all), (off_hbm, off_ref)]
+        )
+    ]
+    for copy in arrive:
+        copy.start()
+    arrive[0].wait()
+
+    def send(c):
+        return pltpu.make_async_copy(
+            out_buf.at[c].reshape(rows, some, cz),
+            out_ref.at[:, c * some : (c + 1) * some],
+            sem.at[c],
+        )
+
+    zero = jnp.zeros((width, cz), BF16)
+    for c in range(width):
+        part = w_ref[c * width : (c + 1) * width, :].astype(BF16)
+        w_mat[2 * c * width : (2 * c + 1) * width, :cz] = part
+        w_mat[2 * c * width : (2 * c + 1) * width, cz:] = zero
+        w_mat[(2 * c + 1) * width : (2 * c + 2) * width, :cz] = zero
+        w_mat[(2 * c + 1) * width : (2 * c + 2) * width, cz:] = part
+
+    for copy in arrive[1:]:
+        copy.wait()
     low = lax.broadcasted_iota(jnp.int32, (total, LANES), 1) < half
     scale = 1.0 / total
     for c in range(chunks):
-        for t in range(n_seq):
-            right_copy(0, 0, c, t).wait_recv()
         for g in range(chunk):
             block = right_all[c, :, g].reshape(total, LANES).astype(F32)
             turned = pltpu.roll(block, half, 1)
@@ -252,18 +291,13 @@
         result = jnp.dot(outer_mat[...], w_mat[...], preferred_element_type=F32)
         for p in range(2 * chunk):
             for h in range(2):
-                col = (c * chunk * 2 + p) * 2 + h
-                out_ref[pl.ds(col, rows, stride=cols), :] = (
-                    result[p * rows : (p + 1) * rows, h * cz : (h + 1) * cz] * scale + off_in[...]
+                col = p * 2 + h
+                out_buf[c, pl.ds(col, rows, stride=some), :] = (
+                    result[p * rows : (p + 1) * rows, h * cz : (h + 1) * cz] * scale + off_ref[...]
                 )
-
-    for k in range(parts):
-        for d in range(2, n_seq, 2):
-            left_copy(d, k, s).wait_send()
-        for d in range(0, n_seq, 2):
-            left_pass(d, k, s).wait_send()
-    for k in range(max(parts - 2, 0), parts):
-        right_sent(k)
+        send(c).start()
+    for c in range(chunks):
+        send(c).wait()
 
 
 def local(n_seq, n_res, features, gain, p1, p2, w, offset):
@@ -281,41 +315,56 @@
     dims = (n_seq, n_res, seqs, rows, cols, width, cz, chunk)
     parts = blocks // chunk
     hbm = pl.BlockSpec(memory_space=pltpu.HBM)
-    out = pl.pallas_call(
+    vmem = pl.BlockSpec(memory_space=pltpu.VMEM)
+    left, right = pl.pallas_call(
         functools.partial(kernel, dims),
-        out_shape=jax.ShapeDtypeStruct((rows * cols, cz), F32),
-        in_specs=[hbm] * 6,
-        out_specs=pl.BlockSpec(memory_space=pltpu.VMEM),
+        out_shape=[
+            jax.ShapeDtypeStruct((width // 2 * rows, 2 * total), BF16),
+            jax.ShapeDtypeStruct((chunks, n_seq, chunk, seqs, LANES), BF16),
+        ],
+        in_specs=[hbm] * 4,
+        out_specs=[vmem] * 2,
         scratch_shapes=[
             pltpu.VMEM((seqs, rows, feats), BF16),
             pltpu.VMEM((1, feats), F32),
             pltpu.VMEM((width, feats), BF16),
             pltpu.VMEM((width, feats), BF16),
-            pltpu.VMEM(w.shape, F32),
-            pltpu.VMEM((1, cz), F32),
             pltpu.VMEM((parts, feats // LANES, seqs * per * chunk, LANES), F32),
             pltpu.VMEM((parts, chunk * seqs, per * feats), BF16),
             pltpu.VMEM((per * feats, 2 * LANES), BF16),
             pltpu.VMEM((parts, n_seq, chunk, seqs, LANES), BF16),
             pltpu.VMEM((parts, chunk, seqs, LANES), BF16),
-            pltpu.VMEM((chunks, n_seq, chunk, seqs, LANES), BF16),
             pltpu.VMEM((total // LANES, rows * width, LANES), F32),
-            pltpu.VMEM((width // 2 * rows, 2 * total), BF16),
-            pltpu.VMEM((2 * total, 2 * LANES), BF16),
-            pltpu.VMEM((chunk * 2 * rows, width // 2 * LANES), BF16),
-            pltpu.VMEM((2 * width * width, 2 * cz), BF16),
             pltpu.SemaphoreType.DMA((n_seq, parts)),
             pltpu.SemaphoreType.DMA((n_seq, parts)),
             pltpu.SemaphoreType.DMA((n_seq, chunks)),
             pltpu.SemaphoreType.DMA((n_seq, chunks)),
             pltpu.SemaphoreType.DMA((parts,)),
-            pltpu.SemaphoreType.DMA((5,)),
+            pltpu.SemaphoreType.DMA((3,)),
         ],
         compiler_params=pltpu.CompilerParams(
             collective_id=0, has_side_effects=True, vmem_limit_bytes=62 * 1024 * 1024
         ),
-    )(features, gain.reshape(1, feats), p1.T, p2.T, w, offset.reshape(1, cz))
-    return out.reshape(rows, cols, cz)
+    )(features, gain.reshape(1, feats), p1.T, p2.T)
+    return pl.pallas_call(
+        functools.partial(pair_kernel, dims),
+        out_shape=jax.ShapeDtypeStruct((rows, cols, cz), F32),
+        in_specs=[hbm] * 4,
+        out_specs=hbm,
+        scratch_shapes=[
+            pltpu.VMEM(left.shape, BF16),
+            pltpu.VMEM(right.shape, BF16),
+            pltpu.VMEM(w.shape, F32),
+            pltpu.VMEM((1, cz), F32),
+            pltpu.VMEM((2 * total, 2 * LANES), BF16),
+            pltpu.VMEM((chunk * 2 * rows, width // 2 * LANES), BF16),
+            pltpu.VMEM((2 * width * width, 2 * cz), BF16),
+            pltpu.VMEM((chunks, rows * (cols // chunks), cz), F32),
+            pltpu.SemaphoreType.DMA((chunks,)),
+            pltpu.SemaphoreType.DMA((4,)),
+        ],
+        compiler_params=pltpu.CompilerParams(vmem_limit_bytes=62 * 1024 * 1024),
+    )(left, right, w, offset.reshape(1, cz))
 
 
 def solution(mesh):

time: 30.5 us -> 28.5 us (0.934)
  the two profiles are of different devices: /device:TPU:1 before, /device:TPU:6 now
where the time goes in v3:
time: 28.5 us; the launch traced here: 28.4 us
  Pallas kernels  28.4 us (100%)
    pallas_call x1, Pallas kernels, local(): pl.pallas_call(functools.partial(kernel, dims), out_shape=[jax.ShapeDtype...  20.2 us
    pallas_call x1, Pallas kernels, local(): pl.pallas_call(functools.partial(pair_kernel, dims), out_shape=jax.ShapeD...  8.13 us

profile of v3, /device:TPU:6, one launch (start us, length us, event | category | flops | bytes accessed | tf_op | source)
XLA Modules:
  0.0 28.4 jit_solution(6190218729190817171)
XLA Ops:
  0.0 20.2 %shard_map.64 = (bf16[1024,256]{1,0:T(8,128)(2,1)}, bf16[4,4,4,32,128]{4,3,2,1,0:T(8,128)(2,1)}) custom-call(bf16[32,64,256]{2,1,0:T(8,128)(2,1)} %x_ref.1, f32[1,256]{1,0:T(1,128)} %bitcast.6, bf16[32,256]{1,0:T(8,128)(2,1)} %bitcast.4, bf16[32,256]{1,0:T(8,128)(2,1)} %bitcast.5), custom_call_target="tpu_custom_call" | custom-call | tf_op jit(solution)/shard_map/pallas_call | solution.py:319
  20.3 8.1 %shard_map.65 = f32[64,64,128]{2,1,0:T(8,128)} custom-call(bf16[1024,256]{1,0:T(8,128)(2,1)} %get-tuple-element.7.left_hbm, bf16[4,4,4,32,128]{4,3,2,1,0:T(8,128)(2,1)} %get-tuple-element.8.right_hbm, f32[1024,128]{1,0:T(8,128)} %w_hbm.1, f32[1,128]{1,0:T(1,128)} %bitcast.7), custom_call_target="tpu_custom_call" | custom-call | tf_op jit(solution)/shard_map/pallas_call | solution.py:349

commit v4 on v3

--- a/solution.py
+++ b/solution.py
@@ -185,17 +185,13 @@
         for d in range(2, n_seq, 2):
             left_copy(d, k, s).start()
         left_pass(0, k, s).start()
-        if k < 2:
-            right_start(k)
+        right_start(k)
 
     for k in range(parts):
         for d in range(2, n_seq, 2):
             source = lax.rem(s + n_seq - d, n_seq)
             left_copy(d, k, source).wait_recv()
             left_pass(d, k, source).start()
-    for k in range(2, parts):
-        right_sent(k - 2)
-        right_start(k)
     for k in range(parts):
         for d in range(0, n_seq, 2):
             left_copy(0, k, lax.rem(s + 1 - 2 * lax.rem(s, 2) + n_seq - d, n_seq)).wait_recv()
@@ -218,7 +214,7 @@
             left_copy(d, k, s).wait_send()
         for d in range(0, n_seq, 2):
             left_pass(d, k, s).wait_send()
-    for k in range(max(parts - 2, 0), parts):
+    for k in range(parts):
         right_sent(k)
 
 

time: 28.5 us -> 26.9 us (0.944)
  the two profiles are of different devices: /device:TPU:6 before, /device:TPU:1 now
where the time goes in v4:
time: 26.9 us; the launch traced here: 26.5 us
  Pallas kernels  26.5 us (99%)
    pallas_call x1, Pallas kernels, local(): pl.pallas_call(functools.partial(kernel, dims), out_shape=[jax.ShapeDtype...  18.3 us
    pallas_call x1, Pallas kernels, local(): pl.pallas_call(functools.partial(pair_kernel, dims), out_shape=jax.ShapeD...  8.13 us

profile of v4, /device:TPU:1, one launch (start us, length us, event | category | flops | bytes accessed | tf_op | source)
XLA Modules:
  0.0 26.5 jit_solution(10372827168627542060)
XLA Ops:
  0.0 18.3 %shard_map.64 = (bf16[1024,256]{1,0:T(8,128)(2,1)}, bf16[4,4,4,32,128]{4,3,2,1,0:T(8,128)(2,1)}) custom-call(bf16[32,64,256]{2,1,0:T(8,128)(2,1)} %x_ref.1, f32[1,256]{1,0:T(1,128)} %bitcast.6, bf16[32,256]{1,0:T(8,128)(2,1)} %bitcast.4, bf16[32,256]{1,0:T(8,128)(2,1)} %bitcast.5), custom_call_target="tpu_custom_call" | custom-call | tf_op jit(solution)/shard_map/pallas_call | solution.py:315
  18.3 8.1 %shard_map.65 = f32[64,64,128]{2,1,0:T(8,128)} custom-call(bf16[1024,256]{1,0:T(8,128)(2,1)} %get-tuple-element.7.left_hbm, bf16[4,4,4,32,128]{4,3,2,1,0:T(8,128)(2,1)} %get-tuple-element.8.right_hbm, f32[1024,128]{1,0:T(8,128)} %w_hbm.1, f32[1,128]{1,0:T(1,128)} %bitcast.7), custom_call_target="tpu_custom_call" | custom-call | tf_op jit(solution)/shard_map/pallas_call | solution.py:345
